TPU v7x, 32 devices: a whole 2x2x4 slice. The times are simulated.
32 devices in a mesh: lat: 8 (over z, x), head: 4 (over y, core).
Axes of the slice: x: 2, y: 2, z: 4, core: 2. Of those that a mesh axis runs over, the one named last changes fastest.
Arguments:
- level_tokens: bfloat16 [4096, 13, 1024], P('lat'), may hold values from -400 to 400
- ln_gain: float32 [1024], replicated, may hold values from 0.25 to 1.75
- key_weight: bfloat16 [1024, 1024], P(None, 'head'), may hold values from -0.1875 to 0.1875
- value_weight: bfloat16 [1024, 1024], P(None, 'head'), may hold values from -0.1875 to 0.1875
- out_weight: bfloat16 [1024, 1024], P('head'), may hold values from -0.1875 to 0.1875
- ocean_queries: bfloat16 [4096, 4, 1024], P('lat', None, 'head'), may hold values from -600 to 600
- send_slots: int32 [8, 8, 64], P('lat'), may hold values from -1 to 511, as said below
Outputs:
- ocean_out: bfloat16 [4096, 4, 1024], P('lat', None, 'head')
Inputs may be any that keep to these rules, and one draw needn't show every extreme that they name: `send_slots`: entry [h, o, k] is a patch index within stripe h, or -1 for an empty slot. The live entries of one stripe are distinct, and in each [h, o] row the live entries come first. In every draw some owner has all 64 slots of every stripe live.
All inputs are finite; a program needn't handle non-finite values.
Results may differ from a plain program's by a relative error of at most 0.013.
The roundings to bfloat16 on the way count: a program that leaves them out, or rounds other values in their place, can miss the bound.
Values may be sent and summed in bfloat16 or wider, within the bound.
No kernel may reach another device: no remote copies, remote signals or barrier semaphores. Data moves between devices by JAX's collectives and lax.ppermute only.
A program may use at most 128 MiB of HBM per device.

v0:
```python
import functools
import math

import jax
import jax.numpy as jnp
from jax import lax
from jax.experimental import pallas as pl
from jax.experimental.pallas import tpu as pltpu
from jax.sharding import PartitionSpec as P

HEAD_DIM = 64
EPS = 1e-05
GROUP = 8
BLOCK = 64
STEP_BLOCKS = 2
STAGE = 128
ROWS = 32
MIB = 1024 * 1024


def params(mib):
    return pltpu.CompilerParams(vmem_limit_bytes=mib * MIB)


def normalize_rows(tokens, gain):
    width = tokens.shape[-1]
    tokens = tokens.astype(jnp.float32)
    center = jnp.sum(tokens, axis=-1, keepdims=True) * (1.0 / width)
    shifted = tokens - center
    spread = jnp.sum(shifted * shifted, axis=-1, keepdims=True) * (1.0 / width)
    return (shifted * lax.rsqrt(spread + EPS) * gain).astype(jnp.bfloat16)


def build_pick(slots_ref, pick_ref, halves):
    stripes, caps = slots_ref.shape
    half = caps // halves
    diagonal = lax.broadcasted_iota(jnp.int32, (caps, caps), 0) == lax.broadcasted_iota(jnp.int32, (caps, caps), 1)
    patch = lax.broadcasted_iota(jnp.int32, (caps, pick_ref.shape[1]), 1)
    for owner in range(stripes):
        row = jnp.broadcast_to(slots_ref[owner : owner + 1, :], (caps, caps))
        column = jnp.sum(jnp.where(diagonal, row, 0), axis=-1, keepdims=True)
        pick = jnp.where(patch == column, 1.0, 0.0).astype(jnp.bfloat16)
        for index in range(halves):
            start = (index * stripes + owner) * half
            pick_ref[start : start + half, :] = pick[index * half : (index + 1) * half]


def project_kernel(
    halves,
    slots_ref,
    gain_ref,
    key_weight_ref,
    value_weight_ref,
    even_ref,
    odd_ref,
    out_ref,
    normed_ref,
    pick_ref,
    weight_ref,
):
    patches = even_ref.shape[1]
    local = key_weight_ref.shape[1]

    @pl.when(pl.program_id(0) == 0)
    def _():
        build_pick(slots_ref, pick_ref, halves)
        weight_ref[:, :local] = key_weight_ref[...]
        weight_ref[:, local:] = value_weight_ref[...]

    gain = gain_ref[...]
    for index, tokens_ref in enumerate((even_ref, odd_ref)):
        for start in range(0, patches, ROWS):
            normed = normalize_rows(tokens_ref[0, pl.ds(start, ROWS), :], gain)
            normed_ref[pl.ds(index * patches + start, ROWS), :] = normed
    product = jnp.dot(normed_ref[...], weight_ref[...], preferred_element_type=jnp.float32).astype(jnp.bfloat16)
    product = jnp.concatenate([product[:patches], product[patches:]], axis=1)
    picked = jnp.dot(pick_ref[...], product, preferred_element_type=jnp.float32)
    groups = picked.shape[0] // GROUP
    picked = [
        picked[:, index * 2 * local : (index + 1) * 2 * local].reshape(groups, 1, GROUP, 2 * local) for index in range(2)
    ]
    picked = jnp.concatenate(picked, axis=1).reshape(out_ref.shape[0], 2 * BLOCK, 2 * local)
    out_ref[:, 0] = picked.astype(jnp.bfloat16)


def project(slots, tokens, gain, key_weight, value_weight, halves):
    levels, patches, width = tokens.shape
    local = key_weight.shape[1]
    count = slots.size
    steps = (levels + 1) // 2
    whole = lambda i: (0, 0)
    return pl.pallas_call(
        functools.partial(project_kernel, halves),
        grid=(steps,),
        in_specs=[
            pl.BlockSpec(slots.shape, whole),
            pl.BlockSpec((1, width), whole),
            pl.BlockSpec((width, local), whole),
            pl.BlockSpec((width, local), whole),
            pl.BlockSpec((1, patches, width), lambda i: (2 * i, 0, 0)),
            pl.BlockSpec((1, patches, width), lambda i: (jnp.minimum(2 * i + 1, levels - 1), 0, 0)),
        ],
        out_specs=pl.BlockSpec((count // BLOCK, 1, 2 * BLOCK, 2 * local), lambda i: (0, i, 0, 0)),
        out_shape=jax.ShapeDtypeStruct((count // BLOCK, steps, 2 * BLOCK, 2 * local), jnp.bfloat16),
        scratch_shapes=[
            pltpu.VMEM((2 * patches, width), jnp.bfloat16),
            pltpu.VMEM((count, patches), jnp.bfloat16),
            pltpu.VMEM((width, 2 * local), jnp.bfloat16),
        ],
        compiler_params=params(58),
        cost_estimate=pl.CostEstimate(
            flops=8 * levels * patches * (width + count) * local,
            bytes_accessed=2 * levels * patches * (width + 2 * local) + 4 * width * local,
            transcendentals=0,
        ),
        name="norm_project",
    )(slots, gain.reshape(1, width), key_weight, value_weight, tokens, tokens)


def attend_kernel(levels, query_ref, pair_ref, *refs):
    out_ref = refs[-1]
    blocks, level_pairs, block, local = pair_ref.shape
    block, local = block // 2, local // 2
    slots = blocks * block
    latents = out_ref.shape[0] // slots
    rows = GROUP * latents
    heads = local // HEAD_DIM
    columns = level_pairs * 2 * GROUP
    lane_head = lax.broadcasted_iota(jnp.int32, (rows, local), 1) // HEAD_DIM
    row_slot = lax.broadcasted_iota(jnp.int32, (GROUP, heads * rows), 0)
    column_slot = (lax.broadcasted_iota(jnp.int32, (GROUP, heads * rows), 1) // latents) & (GROUP - 1)
    same = row_slot - column_slot == 0
    scale = math.log2(math.e) / math.sqrt(HEAD_DIM)
    queries = query_ref[...].reshape(slots * latents, local).astype(jnp.float32)

    def columns_of(start, lane):
        part = pl.ds(start % block * 2, 2 * GROUP)
        return pair_ref[start // block, :, part, pl.ds(lane, local)].reshape(columns, local)

    for first in range(0, slots, STAGE):
        tasks = range(first, first + STAGE, GROUP)
        scores = []
        for start in tasks:
            part = queries[start * latents : start * latents + rows]
            part = jnp.concatenate(
                [jnp.where(lane_head == head, part, 0.0).astype(jnp.bfloat16) for head in range(heads)], axis=0
            )
            product = lax.dot_general(
                columns_of(start, 0), part, (((1,), (1,)), ((), ())), preferred_element_type=jnp.float32
            )
            scores.append(product.reshape(2 * level_pairs, GROUP, heads * rows))
        softs = []
        for product in scores:
            product = product[:levels]
            expo = jnp.exp2((product - jnp.max(product, axis=0, keepdims=True)) * scale)
            inverse = jnp.where(same, 1.0 / jnp.sum(expo, axis=0), 0.0)
            soft = expo * inverse[None]
            if levels < 2 * level_pairs:
                soft = jnp.concatenate([soft, jnp.zeros_like(soft[:1])], axis=0)
            softs.append(soft.reshape(columns, heads * rows).astype(jnp.bfloat16))
        for start, soft in zip(tasks, softs):
            wide = lax.dot_general(
                soft, columns_of(start, local), (((0,), (0,)), ((), ())), preferred_element_type=jnp.float32
            )
            mixed = wide[:rows]
            for head in range(1, heads):
                mixed = jnp.where(lane_head == head, wide[head * rows : (head + 1) * rows], mixed)
            out_ref[pl.ds(start * latents, rows), :] = mixed.astype(jnp.bfloat16)


def attend(queries, pairs, levels, index, after=()):
    stripes, halves, rows, local = queries.shape
    steps = pairs.shape[0] // halves // STEP_BLOCKS
    block = stripes * rows // steps
    pair_shape = (STEP_BLOCKS, *pairs.shape[1:])
    return pl.pallas_call(
        functools.partial(attend_kernel, levels),
        grid=(steps,),
        in_specs=[
            pl.BlockSpec((stripes // steps, 1, rows, local), lambda i: (i, index, 0, 0)),
            pl.BlockSpec(pair_shape, lambda i: (index * steps + i, 0, 0, 0)),
        ]
        + [pl.BlockSpec(memory_space=pl.ANY)] * len(after),
        out_specs=pl.BlockSpec((block, local), lambda i: (i, 0)),
        out_shape=jax.ShapeDtypeStruct((steps * block, local), jnp.bfloat16),
        compiler_params=params(55),
        cost_estimate=pl.CostEstimate(
            flops=1024 * steps * block * levels * local,
            bytes_accessed=4 * steps * (block + levels * STEP_BLOCKS * BLOCK) * local,
            transcendentals=0,
        ),
        name="attend_slots",
    )(queries, pairs, *after)


def combine_rows(mixed_refs, weight_refs, part):
    total = None
    for mixed_ref, weight_ref in zip(mixed_refs, weight_refs):
        term = jnp.dot(mixed_ref[part, :], weight_ref[...], preferred_element_type=jnp.float32)
        term = term.astype(jnp.bfloat16).astype(jnp.float32)
        total = term if total is None else total + term
    return total.astype(jnp.bfloat16)


def combine_home_kernel(place_ref, *refs):
    for distance, out_ref in enumerate(refs[8:]):
        rows = out_ref.shape[0] * out_ref.shape[1]
        start = jnp.bitwise_xor(place_ref[0], distance) * rows
        part = pl.ds(pl.multiple_of(start, rows), rows)
        out_ref[...] = combine_rows(refs[:4], refs[4:8], part).reshape(out_ref.shape)


def combine_kernel(place_ref, *refs):
    out_ref = refs[-1]
    stripes, caps, latents, local = out_ref.shape
    for stripe in range(stripes):
        part = pl.ds(stripe * caps * latents, caps * latents)
        rows = combine_rows(refs[:4], refs[4:8], part)
        out_ref[stripe] = rows.reshape(caps, latents, local)


def term_of(mixed_ref, weight_ref, part):
    term = jnp.dot(mixed_ref[part, :], weight_ref[...], preferred_element_type=jnp.float32)
    return term.astype(jnp.bfloat16).astype(jnp.float32)


def combine_most_kernel(place_ref, *refs):
    out_ref, total_ref = refs[-2:]
    rest = refs[4:-2]
    stripes = out_ref.shape[0]
    half = out_ref.shape[1] - rest[0].shape[0]
    for distance, ref in enumerate(rest):
        out_ref[jnp.bitwise_xor(place_ref[0], distance), half:] = ref[...]
    rows = total_ref.shape[0] // stripes
    for stripe in range(stripes):
        part = pl.ds(stripe * rows, rows)
        total_ref[part, :] = term_of(refs[0], refs[2], part) + term_of(refs[1], refs[3], part)


def combine_last_kernel(first_ref, second_ref, first_weight_ref, second_weight_ref, total_ref, whole_ref, out_ref):
    stripes, half, latents, local = out_ref.shape
    rows = half * latents
    for stripe in range(stripes):
        part = pl.ds(stripe * rows, rows)
        total = total_ref[part, :] + term_of(first_ref, first_weight_ref, part)
        total = total + term_of(second_ref, second_weight_ref, part)
        out_ref[stripe] = total.astype(jnp.bfloat16).reshape(half, latents, local)


def combine_last(mixed, weights, total, whole):
    stripes, caps, latents, local = whole.shape
    half = total.shape[0] // stripes // latents
    operands = (*mixed, *weights, total)
    specs = [pl.BlockSpec(array.shape, lambda i: (0, 0)) for array in operands]
    return pl.pallas_call(
        combine_last_kernel,
        grid=(1,),
        in_specs=specs + [pl.BlockSpec(memory_space=pl.ANY)],
        out_specs=pl.BlockSpec((stripes, half, latents, local), lambda i: (0, 0, 0, 0)),
        out_shape=jax.ShapeDtypeStruct(whole.shape, whole.dtype),
        input_output_aliases={len(operands): 0},
        compiler_params=params(20),
        cost_estimate=pl.CostEstimate(flops=12 * total.size * local, bytes_accessed=10 * total.size, transcendentals=0),
        name="combine_last",
    )(*operands, whole)


def combine(kernel, place, groups, weights, out_shape, rest=()):
    operands = (*groups, *weights, *rest)
    rows, local = groups[0].shape
    vmem = pl.BlockSpec(memory_space=pltpu.VMEM)
    return pl.pallas_call(
        kernel,
        in_specs=[pl.BlockSpec(memory_space=pltpu.SMEM)] + [vmem] * len(operands),
        out_specs=jax.tree.map(lambda _: vmem, out_shape),
        out_shape=out_shape,
        compiler_params=params(20),
        cost_estimate=pl.CostEstimate(
            flops=24 * rows * local * local, bytes_accessed=10 * rows * local, transcendentals=0
        ),
        name="combine_groups",
    )(place, *operands)


def swap(array, axis_name, distance):
    size = lax.axis_size(axis_name)
    return lax.ppermute(array, axis_name, [(i, i ^ distance) for i in range(size)])


def follow(array, *others):
    return lax.optimization_barrier((array, *others))[0]


def spread_heads(mixed, others=()):
    second = swap(mixed, "head", 2)
    return mixed, swap(mixed, "head", 1), second, swap(follow(second, *others), "head", 1)


def exchange(array, stripes):
    array = array.reshape(stripes, -1, *array.shape[1:])
    return lax.all_to_all(array, "lat", split_axis=0, concat_axis=0, tiled=True)


def spread_weight(out_weight, head):
    local = out_weight.shape[0]
    parts = []
    for distance in range(lax.axis_size("head")):
        start = jnp.bitwise_xor(head, distance) * local
        part = lax.dynamic_slice_in_dim(out_weight, start, local, 1)
        parts.append(swap(part, "head", distance) if distance else part)
    return parts


def shards(level_tokens, ln_gain, key_weight, value_weight, out_weight, ocean_queries, send_slots):
    stripes = lax.axis_size("lat")
    caps = send_slots.shape[2]
    shape = ocean_queries.shape
    slots, latents, local = shape
    place = lax.axis_index("lat").reshape(1)
    halves = 2 if caps == BLOCK else 1
    queries = exchange(ocean_queries, stripes).reshape(stripes, halves, -1, local)
    weights = spread_weight(out_weight, lax.axis_index("head"))
    tokens = jnp.transpose(level_tokens, (1, 0, 2))
    levels = tokens.shape[0]
    pairs = project(send_slots[0], tokens, ln_gain, key_weight, value_weight, halves)
    pairs, weights = lax.optimization_barrier((pairs, weights))
    whole = jax.ShapeDtypeStruct((stripes, caps, latents, local), jnp.bfloat16)
    if halves == 1:
        mixed = exchange(attend(queries, pairs, levels, 0), stripes).reshape(-1, local)
        return combine(combine_kernel, place, spread_heads(mixed), weights, whole).reshape(shape)
    late = attend(queries, pairs, levels, 1)
    early = attend(queries, pairs, levels, 0, (late,))
    chunks = [jax.ShapeDtypeStruct((caps // 2, latents, local), jnp.bfloat16)] * stripes
    chunks = combine(combine_home_kernel, place, spread_heads(late, (early,)), weights, chunks)
    order = [*range(stripes // 2 - 1, 0, -1), *range(stripes // 2, stripes)]
    moved = {distance: swap(chunks[distance], "lat", distance) for distance in order}
    near = [moved[distance] for distance in order[: stripes // 2 - 1]]
    far = [moved[distance] for distance in order[stripes // 2 - 1 :]]
    chunks = [chunks[0], *(moved[distance] for distance in range(1, stripes))]
    early = follow(exchange(early, stripes), *near).reshape(-1, local)
    own, across, second, third = spread_heads(early, far)
    most_shape = (whole, jax.ShapeDtypeStruct(early.shape, jnp.float32))
    out, total = combine(combine_most_kernel, place, (own, second), weights[::2], most_shape, chunks)
    return combine_last((across, third), weights[1::2], total, out).reshape(shape)


def solution(mesh):
    return jax.shard_map(
        shards,
        mesh=mesh,
        in_specs=(
            P("lat", None, None),
            P(),
            P(None, "head"),
            P(None, "head"),
            P("head", None),
            P("lat", None, "head"),
            P("lat", None, None),
        ),
        out_specs=P("lat", None, "head"),
        check_vma=False,
    )
```

profile of v0, /device:TPU:0, one launch (start us, length us, event | category | flops | bytes accessed | tf_op | source)
XLA Modules:
  0.0 81.8 jit_solution(10211006728132267986)
XLA Ops:
  0.0 7.3 %all-to-all-start = ((bf16[8,64,4,256]{3,2,1,0:T(4,128)(2,1)}), bf16[8,64,4,256]{3,2,1,0:T(4,128)(2,1)S(1)}, u32[]{:S(2)}, u32[]{:S(2)}) async-start(bf16[8,64,4,256]{3,2,1,0:T(4,128)(2,1)} %bitcast.11), calls=%async_computation | async-start | bytes 2097152 | tf_op jit(solution)/shard_map/all_to_all | solution.py:301
  7.3 1.1 %constant_dynamic-slice_fusion = (bf16[256,256]{1,0:T(8,128)(2,1)S(1)}, bf16[256,256]{1,0:T(8,128)(2,1)S(1)}, bf16[256,256]{1,0:T(8,128)(2,1)S(1)}, bf16[256,256]{1,0:T(8,128)(2,1)S(1)}) fusion(bf16[256,1024]{1,0:T(8,128)(2,1)} %param.11, s32[]{:T(128)S(6)} %select_n.15, s32[]{:T(128)S(6)} %select_n.13, s32[]{:T(128)S(6)} %select_n.12, s32[]{:T(128)S(6)} %select_n.14), kind=kLoop, calls=%fused_computation | loop fusion | bytes 1048592 | tf_op jit(solution)/shard_map/dynamic_slice | solution.py:309
  8.4 0.7 collective-permute-start.2
  9.1 1.0 %collective-permute-start = (bf16[256,256]{1,0:T(8,128)(2,1)S(1)}, bf16[256,256]{1,0:T(8,128)(2,1)S(1)}, u32[]{:S(2)}, u32[]{:S(2)}) collective-permute-start(bf16[256,256]{1,0:T(8,128)(2,1)S(1)} %get-tuple-element.42), channel_id=1, source_target_pairs={{0,1},{1,0},{2,3},{3,2},{4,5},{5,4},{6,7},{7,6},{8,9},{9,8},{10,11... | collective-permute-start | bytes 393224 | tf_op jit(solution)/shard_map/ppermute | solution.py:287
  10.1 0.5 collective-permute-start.1
  10.6 21.9 %norm_project.1.pair_ref = bf16[8,7,128,512]{3,2,1,0:T(8,128)(2,1)} custom-call(s32[8,64]{1,0:T(8,128)} %bitcast.15, f32[1,1024]{1,0:T(1,128)} %bitcast.16, bf16[1024,256]{1,0:T(8,128)(2,1)} %key_weight_ref.1, bf16[1024,256]{1,0:T(8,128)(2,1)} %value_weight_ref.1, bf16[13,512,1024]{2,1,0:T(8,128)(2,1)} %bitcast.13, bf16[13,512,1024]{2,1,0:T(8,128)(2,1)} %bitcast.14), custom_call_target="tpu_custom_call" | custom-call | flops 20937965568 | bytes 21495808 | tf_op jit(solution)/shard_map/norm_project/pallas_call | solution.py:92
  32.6 0.5 all-to-all-done
  33.0 1.1 %reshape.22.query_ref = bf16[8,2,128,256]{3,2,1,0:T(8,128)(2,1)} reshape(bf16[8,64,4,256]{3,2,1,0:T(4,128)(2,1)S(1)} %all-to-all-done) | data formatting | bytes 2097152 | tf_op jit(solution)/shard_map/reshape | solution.py:321
  34.1 3.8 %attend_slots.2.refs_0_ = bf16[1024,256]{1,0:T(8,128)(2,1)} custom-call(bf16[8,2,128,256]{3,2,1,0:T(8,128)(2,1)} %reshape.22.query_ref, bf16[8,7,128,512]{3,2,1,0:T(8,128)(2,1)} %norm_project.1.pair_ref), custom_call_target="tpu_custom_call" | custom-call | flops 3489660928 | bytes 4456448 | tf_op jit(solution)/shard_map/attend_slots/pallas_call | solution.py:176
  38.0 1.5 %collective-permute-start.4 = (bf16[1024,256]{1,0:T(8,128)(2,1)}, bf16[1024,256]{1,0:T(8,128)(2,1)S(1)}, u32[]{:S(2)}, u32[]{:S(2)}) collective-permute-start(bf16[1024,256]{1,0:T(8,128)(2,1)} %attend_slots.2.refs_0_), channel_id=1, source_target_pairs={{0,2},{1,3},{2,0},{3,1},{4,6},{5,7},{6,4},{7,5},{8,10},{9,11},{10,... | collective-permute-start | bytes 1572872 | tf_op jit(solution)/shard_map/ppermute | solution.py:287
  39.5 3.8 %attend_slots.3 = bf16[1024,256]{1,0:T(8,128)(2,1)} custom-call(bf16[8,2,128,256]{3,2,1,0:T(8,128)(2,1)} %reshape.22.query_ref, bf16[8,7,128,512]{3,2,1,0:T(8,128)(2,1)} %norm_project.1.pair_ref, bf16[1024,256]{1,0:T(8,128)(2,1)} %attend_slots.2.refs_0_), custom_call_target="tpu_custom_call" | custom-call | flops 3489660928 | bytes 4456448 | tf_op jit(solution)/shard_map/attend_slots/pallas_call | solution.py:176
  43.3 5.6 %all-to-all-start.1 = ((bf16[8,128,256]{2,1,0:T(8,128)(2,1)}), bf16[8,128,256]{2,1,0:T(8,128)(2,1)S(1)}, u32[]{:S(2)}, u32[]{:S(2)}) async-start(bf16[8,128,256]{2,1,0:T(8,128)(2,1)} %bitcast.12), calls=%async_computation.1 | async-start | bytes 1048576 | tf_op jit(solution)/shard_map/all_to_all | solution.py:301
  48.8 0.1 collective-permute-start.3
  48.9 2.4 %collective-permute-done.4.refs_2_ = bf16[1024,256]{1,0:T(8,128)(2,1)S(1)} collective-permute-done((bf16[1024,256]{1,0:T(8,128)(2,1)}, bf16[1024,256]{1,0:T(8,128)(2,1)S(1)}, u32[]{:S(2)}, u32[]{:S(2)}) %collective-permute-start.4) | collective-permute-done | bytes 524320 | tf_op jit(solution)/shard_map/ppermute | solution.py:287
  51.3 1.9 %collective-permute-done.5.refs_3_ = bf16[1024,256]{1,0:T(8,128)(2,1)S(1)} collective-permute-done((bf16[1024,256]{1,0:T(8,128)(2,1)S(1)}, bf16[1024,256]{1,0:T(8,128)(2,1)S(1)}, u32[]{:S(2)}, u32[]{:S(2)}) %collective-permute-start.5) | collective-permute-done | bytes 524320 | tf_op jit(solution)/shard_map/ppermute | solution.py:287
  53.2 1.2 %combine_groups.2 = (bf16[32,4,256]{2,1,0:T(4,128)(2,1)S(1)}, bf16[32,4,256]{2,1,0:T(4,128)(2,1)S(1)}, bf16[32,4,256]{2,1,0:T(4,128)(2,1)S(1)}, bf16[32,4,256]{2...) custom-call(s32[1]{0:T(128)} %bitcast.5.place_ref, ...), custom_call_target="tpu_custom_call" | custom-call | flops 1610612736 | bytes 2621440 | tf_op jit(solution)/shard_map/combine_groups/pallas_call | solution.py:272
  54.4 0.6 copy-done.1
  55.0 2.9 %collective-permute-start.6 = (bf16[32,4,256]{2,1,0:T(4,128)(2,1)}, bf16[32,4,256]{2,1,0:T(4,128)(2,1)S(1)}, u32[]{:S(2)}, u32[]{:S(2)}) collective-permute-start(bf16[32,4,256]{2,1,0:T(4,128)(2,1)} %get-tuple-element.29), channel_id=1, source_target_pairs={{0,12},{4,8},{8,4},{12,0},{16,28},{20,24},{24,20},{28,16},{1,13},{... | collective-permute-start | bytes 196616 | tf_op jit(solution)/shard_map/ppermute | solution.py:287
  58.0 0.6 collective-permute-start.7
  58.5 4.5 %all-to-all-done.1 = bf16[8,128,256]{2,1,0:T(8,128)(2,1)S(1)} async-done(((bf16[8,128,256]{2,1,0:T(8,128)(2,1)}), bf16[8,128,256]{2,1,0:T(8,128)(2,1)S(1)}, u32[]{:S(2)}, u32[]{:S(2)}) %all-to-all-start.1) | async-done | bytes 524320 | tf_op jit(solution)/shard_map/all_to_all | solution.py:301
  63.1 0.9 %collective-permute-done.7.refs_6_ = bf16[32,4,256]{2,1,0:T(4,128)(2,1)S(1)} collective-permute-done((bf16[32,4,256]{2,1,0:T(4,128)(2,1)S(1)}, bf16[32,4,256]{2,1,0:T(4,128)(2,1)S(1)}, u32[]{:S(2)}, u32[]{:S(2)}) %collective-permute-start.7) | collective-permute-done | bytes 65568 | tf_op jit(solution)/shard_map/ppermute | solution.py:287
  63.9 1.4 %collective-permute-start.10 = (bf16[1024,256]{1,0:T(8,128)(2,1)S(1)}, bf16[1024,256]{1,0:T(8,128)(2,1)S(1)}, u32[]{:S(2)}, u32[]{:S(2)}) collective-permute-start(bf16[1024,256]{1,0:T(8,128)(2,1)S(1)} %bitcast.8), channel_id=1, source_target_pairs={{0,2},{1,3},{2,0},{3,1},{4,6},{5,7},{6,4},{7,5},{8,10},{9,11},{10,... | collective-permute-start | bytes 1572872 | tf_op jit(solution)/shard_map/ppermute | solution.py:287
  65.3 1.4 %collective-permute-start.11 = (bf16[32,4,256]{2,1,0:T(4,128)(2,1)S(1)}, bf16[32,4,256]{2,1,0:T(4,128)(2,1)S(1)}, u32[]{:S(2)}, u32[]{:S(2)}) collective-permute-start(bf16[32,4,256]{2,1,0:T(4,128)(2,1)S(1)} %get-tuple-element.33), channel_id=1, source_target_pairs={{0,16},{4,20},{8,24},{12,28},{16,0},{20,4},{24,8},{28,12},{1,17},{... | collective-permute-start | bytes 196616 | tf_op jit(solution)/shard_map/ppermute | solution.py:287
  66.7 1.7 %collective-permute-start.12 = (bf16[32,4,256]{2,1,0:T(4,128)(2,1)S(1)}, bf16[32,4,256]{2,1,0:T(4,128)(2,1)S(1)}, u32[]{:S(2)}, u32[]{:S(2)}) collective-permute-start(bf16[32,4,256]{2,1,0:T(4,128)(2,1)S(1)} %get-tuple-element.34), channel_id=1, source_target_pairs={{0,20},{4,16},{8,28},{12,24},{16,4},{20,0},{24,12},{28,8},{1,21},{... | collective-permute-start | bytes 196616 | tf_op jit(solution)/shard_map/ppermute | solution.py:287
  68.4 2.9 %collective-permute-start.13 = (bf16[32,4,256]{2,1,0:T(4,128)(2,1)S(1)}, bf16[32,4,256]{2,1,0:T(4,128)(2,1)S(1)}, u32[]{:S(2)}, u32[]{:S(2)}) collective-permute-start(bf16[32,4,256]{2,1,0:T(4,128)(2,1)S(1)} %get-tuple-element.35), channel_id=1, source_target_pairs={{0,24},{4,28},{8,16},{12,20},{16,8},{20,12},{24,0},{28,4},{1,25},{... | collective-permute-start | bytes 196616 | tf_op jit(solution)/shard_map/ppermute | solution.py:287
  71.3 1.7 %collective-permute-start.14 = (bf16[32,4,256]{2,1,0:T(4,128)(2,1)S(1)}, bf16[32,4,256]{2,1,0:T(4,128)(2,1)S(1)}, u32[]{:S(2)}, u32[]{:S(2)}) collective-permute-start(bf16[32,4,256]{2,1,0:T(4,128)(2,1)S(1)} %get-tuple-element.36), channel_id=1, source_target_pairs={{0,28},{4,24},{8,20},{12,16},{16,12},{20,8},{24,4},{28,0},{1,29},{... | collective-permute-start | bytes 196616 | tf_op jit(solution)/shard_map/ppermute | solution.py:287
  73.0 2.4 %collective-permute-done.11.refs_8_ = bf16[32,4,256]{2,1,0:T(4,128)(2,1)S(1)} collective-permute-done((bf16[32,4,256]{2,1,0:T(4,128)(2,1)S(1)}, bf16[32,4,256]{2,1,0:T(4,128)(2,1)S(1)}, u32[]{:S(2)}, u32[]{:S(2)}) %collective-permute-start.11) | collective-permute-done | bytes 65568 | tf_op jit(solution)/shard_map/ppermute | solution.py:287
  75.4 1.6 %collective-permute-done.12.refs_9_ = bf16[32,4,256]{2,1,0:T(4,128)(2,1)S(1)} collective-permute-done((bf16[32,4,256]{2,1,0:T(4,128)(2,1)S(1)}, bf16[32,4,256]{2,1,0:T(4,128)(2,1)S(1)}, u32[]{:S(2)}, u32[]{:S(2)}) %collective-permute-start.12) | collective-permute-done | bytes 65568 | tf_op jit(solution)/shard_map/ppermute | solution.py:287
  77.0 1.3 %collective-permute-done.14.refs_11_ = bf16[32,4,256]{2,1,0:T(4,128)(2,1)S(1)} collective-permute-done((bf16[32,4,256]{2,1,0:T(4,128)(2,1)S(1)}, bf16[32,4,256]{2,1,0:T(4,128)(2,1)S(1)}, u32[]{:S(2)}, u32[]{:S(2)}) %collective-permute-start.14) | collective-permute-done | bytes 65568 | tf_op jit(solution)/shard_map/ppermute | solution.py:287
  78.3 0.8 %copy-done.2 = bf16[32,4,256]{2,1,0:T(4,128)(2,1)S(1)} copy-done((bf16[32,4,256]{2,1,0:T(4,128)(2,1)S(1)}, bf16[32,4,256]{2,1,0:T(4,128)(2,1)}, u32[]{:S(2)}) %copy-start.2) | copy-done | bytes 65560
  79.2 1.4 %combine_groups.3 = (bf16[8,64,4,256]{3,2,1,0:T(4,128)(2,1)}, f32[1024,256]{1,0:T(8,128)S(1)}) custom-call(s32[1]{0:T(128)} %bitcast.5.place_ref, bf16[1024,256]{1,0:T(8,128)(2,1)S(1)} %bitcast.10, bf16[1024,256]{1,0:T(8,128)(2,1)S(1)} %collective-permute-done.10.refs_1_, bf16[256,256]{1,0:T(8,128)(2,1)S(1)} %get-tuple-element.25.refs_4_.refs_2_, ...), custom_call_target="tpu_custom_call" | custom-call | flops 1610612736 | bytes 2621440 | tf_op jit(solution)/shard_map/combine_groups/pallas_call | solution.py:272
  80.6 1.2 %combine_last.1 = bf16[8,64,4,256]{3,2,1,0:T(4,128)(2,1)} custom-call(bf16[1024,256]{1,0:T(8,128)(2,1)S(1)} %collective-permute-done.9.first_ref, bf16[1024,256]{1,0:T(8,128)(2,1)S(1)} %collective-permute-done.15.second_ref, bf16[256,256]{1,0:T(8,128)(2,1)S(1)} %collective-permute-done.refs_5_.first_weight_ref, ...), custom_call_target="tpu_custom_call", output_to_operand_aliasing={{}: (5, {})} | custom-call | flops 805306368 | bytes 2621440 | tf_op jit(solution)/shard_map/combine_last/pallas_call | solution.py:255
  (18 shorter events, 0.0 us)
Async XLA Ops:
  0.0 33.0 %all-to-all-start = ((bf16[8,64,4,256]{3,2,1,0:T(4,128)(2,1)}), bf16[8,64,4,256]{3,2,1,0:T(4,128)(2,1)S(1)}, u32[]{:S(2)}, u32[]{:S(2)}) async-start(bf16[8,64,4,256]{3,2,1,0:T(4,128)(2,1)} %bitcast.11), calls=%async_computation | async-start | bytes 2097152 | tf_op jit(solution)/shard_map/all_to_all | solution.py:301
  8.4 24.2 %collective-permute-start.2 = (bf16[256,256]{1,0:T(8,128)(2,1)S(1)}, bf16[256,256]{1,0:T(8,128)(2,1)S(1)}, u32[]{:S(2)}, u32[]{:S(2)}) collective-permute-start(bf16[256,256]{1,0:T(8,128)(2,1)S(1)} %get-tuple-element.41), channel_id=1, source_target_pairs={{0,3},{1,2},{2,1},{3,0},{4,7},{5,6},{6,5},{7,4},{8,11},{9,10},{10,... | collective-permute-start | bytes 393224 | tf_op jit(solution)/shard_map/ppermute | solution.py:287
  9.1 23.4 %collective-permute-start = (bf16[256,256]{1,0:T(8,128)(2,1)S(1)}, bf16[256,256]{1,0:T(8,128)(2,1)S(1)}, u32[]{:S(2)}, u32[]{:S(2)}) collective-permute-start(bf16[256,256]{1,0:T(8,128)(2,1)S(1)} %get-tuple-element.42), channel_id=1, source_target_pairs={{0,1},{1,0},{2,3},{3,2},{4,5},{5,4},{6,7},{7,6},{8,9},{9,8},{10,11... | collective-permute-start | bytes 393224 | tf_op jit(solution)/shard_map/ppermute | solution.py:287
  10.1 22.5 %collective-permute-start.1 = (bf16[256,256]{1,0:T(8,128)(2,1)S(1)}, bf16[256,256]{1,0:T(8,128)(2,1)S(1)}, u32[]{:S(2)}, u32[]{:S(2)}) collective-permute-start(bf16[256,256]{1,0:T(8,128)(2,1)S(1)} %get-tuple-element.44), channel_id=1, source_target_pairs={{0,2},{1,3},{2,0},{3,1},{4,6},{5,7},{6,4},{7,5},{8,10},{9,11},{10,... | collective-permute-start | bytes 393224 | tf_op jit(solution)/shard_map/ppermute | solution.py:287
  38.0 10.9 %copy-start = (bf16[1024,256]{1,0:T(8,128)(2,1)S(1)}, bf16[1024,256]{1,0:T(8,128)(2,1)}, u32[]{:S(2)}) copy-start(bf16[1024,256]{1,0:T(8,128)(2,1)} %attend_slots.2.refs_0_) | copy-start | bytes 1572868
  38.0 13.3 %collective-permute-start.4 = (bf16[1024,256]{1,0:T(8,128)(2,1)}, bf16[1024,256]{1,0:T(8,128)(2,1)S(1)}, u32[]{:S(2)}, u32[]{:S(2)}) collective-permute-start(bf16[1024,256]{1,0:T(8,128)(2,1)} %attend_slots.2.refs_0_), channel_id=1, source_target_pairs={{0,2},{1,3},{2,0},{3,1},{4,6},{5,7},{6,4},{7,5},{8,10},{9,11},{10,... | collective-permute-start | bytes 1572872 | tf_op jit(solution)/shard_map/ppermute | solution.py:287
  43.3 19.8 %all-to-all-start.1 = ((bf16[8,128,256]{2,1,0:T(8,128)(2,1)}), bf16[8,128,256]{2,1,0:T(8,128)(2,1)S(1)}, u32[]{:S(2)}, u32[]{:S(2)}) async-start(bf16[8,128,256]{2,1,0:T(8,128)(2,1)} %bitcast.12), calls=%async_computation.1 | async-start | bytes 1048576 | tf_op jit(solution)/shard_map/all_to_all | solution.py:301
  48.8 2.5 %collective-permute-start.3 = (bf16[1024,256]{1,0:T(8,128)(2,1)S(1)}, bf16[1024,256]{1,0:T(8,128)(2,1)S(1)}, u32[]{:S(2)}, u32[]{:S(2)}) collective-permute-start(bf16[1024,256]{1,0:T(8,128)(2,1)S(1)} %copy-done), channel_id=1, source_target_pairs={{0,1},{1,0},{2,3},{3,2},{4,5},{5,4},{6,7},{7,6},{8,9},{9,8},{10,11... | collective-permute-start | bytes 1572872 | tf_op jit(solution)/shard_map/ppermute | solution.py:287
  51.3 1.9 %collective-permute-start.5 = (bf16[1024,256]{1,0:T(8,128)(2,1)S(1)}, bf16[1024,256]{1,0:T(8,128)(2,1)S(1)}, u32[]{:S(2)}, u32[]{:S(2)}) collective-permute-start(bf16[1024,256]{1,0:T(8,128)(2,1)S(1)} %collective-permute-done.4.refs_2_), channel_id=1, source_target_pairs={{0,1},{1,0},{2,3},{3,2},{4,5},{5,4},{6,7},{7,6},{8,9},{9,8},{10,11... | collective-permute-start | bytes 1572872 | tf_op jit(solution)/shard_map/ppermute | solution.py:287
  54.4 0.6 copy-start.1
  55.0 8.0 %collective-permute-start.6 = (bf16[32,4,256]{2,1,0:T(4,128)(2,1)}, bf16[32,4,256]{2,1,0:T(4,128)(2,1)S(1)}, u32[]{:S(2)}, u32[]{:S(2)}) collective-permute-start(bf16[32,4,256]{2,1,0:T(4,128)(2,1)} %get-tuple-element.29), channel_id=1, source_target_pairs={{0,12},{4,8},{8,4},{12,0},{16,28},{20,24},{24,20},{28,16},{1,13},{... | collective-permute-start | bytes 196616 | tf_op jit(solution)/shard_map/ppermute | solution.py:287
  58.0 6.0 %collective-permute-start.7 = (bf16[32,4,256]{2,1,0:T(4,128)(2,1)S(1)}, bf16[32,4,256]{2,1,0:T(4,128)(2,1)S(1)}, u32[]{:S(2)}, u32[]{:S(2)}) collective-permute-start(bf16[32,4,256]{2,1,0:T(4,128)(2,1)S(1)} %get-tuple-element.30), channel_id=1, source_target_pairs={{0,8},{4,12},{8,0},{12,4},{16,24},{20,28},{24,16},{28,20},{1,9},{5... | collective-permute-start | bytes 196616 | tf_op jit(solution)/shard_map/ppermute | solution.py:287
  58.5 5.4 %collective-permute-start.8 = (bf16[32,4,256]{2,1,0:T(4,128)(2,1)S(1)}, bf16[32,4,256]{2,1,0:T(4,128)(2,1)S(1)}, u32[]{:S(2)}, u32[]{:S(2)}) collective-permute-start(bf16[32,4,256]{2,1,0:T(4,128)(2,1)S(1)} %get-tuple-element.31), channel_id=1, source_target_pairs={{0,4},{4,0},{8,12},{12,8},{16,20},{20,16},{24,28},{28,24},{1,5},{5... | collective-permute-start | bytes 196616 | tf_op jit(solution)/shard_map/ppermute | solution.py:287
  63.9 14.4 %collective-permute-start.10 = (bf16[1024,256]{1,0:T(8,128)(2,1)S(1)}, bf16[1024,256]{1,0:T(8,128)(2,1)S(1)}, u32[]{:S(2)}, u32[]{:S(2)}) collective-permute-start(bf16[1024,256]{1,0:T(8,128)(2,1)S(1)} %bitcast.8), channel_id=1, source_target_pairs={{0,2},{1,3},{2,0},{3,1},{4,6},{5,7},{6,4},{7,5},{8,10},{9,11},{10,... | collective-permute-start | bytes 1572872 | tf_op jit(solution)/shard_map/ppermute | solution.py:287
  65.3 10.1 %collective-permute-start.11 = (bf16[32,4,256]{2,1,0:T(4,128)(2,1)S(1)}, bf16[32,4,256]{2,1,0:T(4,128)(2,1)S(1)}, u32[]{:S(2)}, u32[]{:S(2)}) collective-permute-start(bf16[32,4,256]{2,1,0:T(4,128)(2,1)S(1)} %get-tuple-element.33), channel_id=1, source_target_pairs={{0,16},{4,20},{8,24},{12,28},{16,0},{20,4},{24,8},{28,12},{1,17},{... | collective-permute-start | bytes 196616 | tf_op jit(solution)/shard_map/ppermute | solution.py:287
  66.7 10.3 %collective-permute-start.12 = (bf16[32,4,256]{2,1,0:T(4,128)(2,1)S(1)}, bf16[32,4,256]{2,1,0:T(4,128)(2,1)S(1)}, u32[]{:S(2)}, u32[]{:S(2)}) collective-permute-start(bf16[32,4,256]{2,1,0:T(4,128)(2,1)S(1)} %get-tuple-element.34), channel_id=1, source_target_pairs={{0,20},{4,16},{8,28},{12,24},{16,4},{20,0},{24,12},{28,8},{1,21},{... | collective-permute-start | bytes 196616 | tf_op jit(solution)/shard_map/ppermute | solution.py:287
  68.4 8.6 %collective-permute-start.13 = (bf16[32,4,256]{2,1,0:T(4,128)(2,1)S(1)}, bf16[32,4,256]{2,1,0:T(4,128)(2,1)S(1)}, u32[]{:S(2)}, u32[]{:S(2)}) collective-permute-start(bf16[32,4,256]{2,1,0:T(4,128)(2,1)S(1)} %get-tuple-element.35), channel_id=1, source_target_pairs={{0,24},{4,28},{8,16},{12,20},{16,8},{20,12},{24,0},{28,4},{1,25},{... | collective-permute-start | bytes 196616 | tf_op jit(solution)/shard_map/ppermute | solution.py:287
  71.3 7.1 %collective-permute-start.14 = (bf16[32,4,256]{2,1,0:T(4,128)(2,1)S(1)}, bf16[32,4,256]{2,1,0:T(4,128)(2,1)S(1)}, u32[]{:S(2)}, u32[]{:S(2)}) collective-permute-start(bf16[32,4,256]{2,1,0:T(4,128)(2,1)S(1)} %get-tuple-element.36), channel_id=1, source_target_pairs={{0,28},{4,24},{8,20},{12,16},{16,12},{20,8},{24,4},{28,0},{1,29},{... | collective-permute-start | bytes 196616 | tf_op jit(solution)/shard_map/ppermute | solution.py:287
  75.4 5.2 %collective-permute-start.9 = (bf16[1024,256]{1,0:T(8,128)(2,1)S(1)}, bf16[1024,256]{1,0:T(8,128)(2,1)S(1)}, u32[]{:S(2)}, u32[]{:S(2)}) collective-permute-start(bf16[1024,256]{1,0:T(8,128)(2,1)S(1)} %bitcast.9), channel_id=1, source_target_pairs={{0,1},{1,0},{2,3},{3,2},{4,5},{5,4},{6,7},{7,6},{8,9},{9,8},{10,11... | collective-permute-start | bytes 1572872 | tf_op jit(solution)/shard_map/ppermute | solution.py:287
  78.3 2.2 %collective-permute-start.15 = (bf16[1024,256]{1,0:T(8,128)(2,1)S(1)}, bf16[1024,256]{1,0:T(8,128)(2,1)S(1)}, u32[]{:S(2)}, u32[]{:S(2)}) collective-permute-start(bf16[1024,256]{1,0:T(8,128)(2,1)S(1)} %collective-permute-done.10.refs_1_), channel_id=1, source_target_pairs={{0,1},{1,0},{2,3},{3,2},{4,5},{5,4},{6,7},{7,6},{8,9},{9,8},{10,11... | collective-permute-start | bytes 1572872 | tf_op jit(solution)/shard_map/ppermute | solution.py:287
  78.3 0.8 %copy-start.2 = (bf16[32,4,256]{2,1,0:T(4,128)(2,1)S(1)}, bf16[32,4,256]{2,1,0:T(4,128)(2,1)}, u32[]{:S(2)}) copy-start(bf16[32,4,256]{2,1,0:T(4,128)(2,1)} %copy-done.1) | copy-start | bytes 196612
where the time goes:
time: 82.2 us; the launch traced here: 81.8 us
  Pallas kernels  33.4 us (41%)
  starting transfers between devices  29.1 us (35%)
  waiting for transfers between devices  15.5 us (19%)
  local copies, waits for them, and re-layouts  3.68 us (4%)
    pallas_call x1, Pallas kernels, project(): pl.pallas_call(functools.partial(project_kernel, halves), grid=(steps,),...  21.9 us
    ppermute x16, starting transfers between devices, swap(): lax.ppermute(array, axis_name, [(i, i ^ distance) for i in range(size)])  16.3 us
    all_to_all x2, starting transfers between devices, exchange(): return lax.all_to_all(array, 'lat', split_axis=0, concat_axis=0, tiled=True)  12.8 us
    ppermute x16, waiting for transfers between devices, swap(): lax.ppermute(array, axis_name, [(i, i ^ distance) for i in range(size)])  10.5 us
    pallas_call x2, Pallas kernels, attend(): pl.pallas_call(functools.partial(attend_kernel, levels), grid=(steps,), i...  7.63 us
    all_to_all x2, waiting for transfers between devices, exchange(): return lax.all_to_all(array, 'lat', split_axis=0, concat_axis=0, tiled=True)  4.97 us
    pallas_call x2, Pallas kernels, combine(): pl.pallas_call(kernel, in_specs=[pl.BlockSpec(memory_space=pltpu.SMEM)] +...  2.61 us
  transfers between devices with their start and end apart: 18, of which 8 were waited for; matrix products, arithmetic and copies ran while one was open for 1% of the time, Pallas kernels for 35%

commit v1 on v0

--- a/solution.py
+++ b/solution.py
@@ -47,6 +47,7 @@
 
 def project_kernel(
     halves,
+    levels,
     slots_ref,
     gain_ref,
     key_weight_ref,
@@ -67,20 +68,38 @@
         weight_ref[:, :local] = key_weight_ref[...]
         weight_ref[:, local:] = value_weight_ref[...]
 
-    gain = gain_ref[...]
-    for index, tokens_ref in enumerate((even_ref, odd_ref)):
-        for start in range(0, patches, ROWS):
-            normed = normalize_rows(tokens_ref[0, pl.ds(start, ROWS), :], gain)
-            normed_ref[pl.ds(index * patches + start, ROWS), :] = normed
-    product = jnp.dot(normed_ref[...], weight_ref[...], preferred_element_type=jnp.float32).astype(jnp.bfloat16)
-    product = jnp.concatenate([product[:patches], product[patches:]], axis=1)
-    picked = jnp.dot(pick_ref[...], product, preferred_element_type=jnp.float32)
-    groups = picked.shape[0] // GROUP
-    picked = [
-        picked[:, index * 2 * local : (index + 1) * 2 * local].reshape(groups, 1, GROUP, 2 * local) for index in range(2)
-    ]
-    picked = jnp.concatenate(picked, axis=1).reshape(out_ref.shape[0], 2 * BLOCK, 2 * local)
-    out_ref[:, 0] = picked.astype(jnp.bfloat16)
+    def multiply(tokens_refs):
+        gain = gain_ref[...]
+        count = len(tokens_refs)
+        for index, tokens_ref in enumerate(tokens_refs):
+            for start in range(0, patches, ROWS):
+                normed = normalize_rows(tokens_ref[0, pl.ds(start, ROWS), :], gain)
+                normed_ref[pl.ds(index * patches + start, ROWS), :] = normed
+        normed = normed_ref[pl.ds(0, count * patches), :]
+        product = jnp.dot(normed, weight_ref[...], preferred_element_type=jnp.float32).astype(jnp.bfloat16)
+        product = jnp.concatenate([product[i * patches : (i + 1) * patches] for i in range(count)], axis=1)
+        picked = jnp.dot(pick_ref[...], product, preferred_element_type=jnp.float32)
+        groups = picked.shape[0] // GROUP
+        picked = [
+            picked[:, i * 2 * local : (i + 1) * 2 * local].reshape(groups, 1, GROUP, 2 * local) for i in range(count)
+        ]
+        if count == 1:
+            picked.append(jnp.zeros_like(picked[0]))
+        picked = jnp.concatenate(picked, axis=1).reshape(out_ref.shape[0], 2 * BLOCK, 2 * local)
+        out_ref[:, 0] = picked.astype(jnp.bfloat16)
+
+    single = levels % 2 == 1
+    last = pl.num_programs(0) - 1
+
+    @pl.when((pl.program_id(0) < last) | (not single))
+    def _():
+        multiply((even_ref, odd_ref))
+
+    if single:
+
+        @pl.when(pl.program_id(0) == last)
+        def _():
+            multiply((even_ref,))
 
 
 def project(slots, tokens, gain, key_weight, value_weight, halves):
@@ -90,7 +109,7 @@
     steps = (levels + 1) // 2
     whole = lambda i: (0, 0)
     return pl.pallas_call(
-        functools.partial(project_kernel, halves),
+        functools.partial(project_kernel, halves, levels),
         grid=(steps,),
         in_specs=[
             pl.BlockSpec(slots.shape, whole),
@@ -332,11 +351,10 @@
     early = attend(queries, pairs, levels, 0, (late,))
     chunks = [jax.ShapeDtypeStruct((caps // 2, latents, local), jnp.bfloat16)] * stripes
     chunks = combine(combine_home_kernel, place, spread_heads(late, (early,)), weights, chunks)
-    order = [*range(stripes // 2 - 1, 0, -1), *range(stripes // 2, stripes)]
+    order = [*range(1, stripes // 2), *range(stripes - 1, stripes // 2 - 1, -1)]
     moved = {distance: swap(chunks[distance], "lat", distance) for distance in order}
-    near = [moved[distance] for distance in order[: stripes // 2 - 1]]
-    far = [moved[distance] for distance in order[stripes // 2 - 1 :]]
     chunks = [chunks[0], *(moved[distance] for distance in range(1, stripes))]
+    near, far = chunks[: stripes // 2], [moved[distance] for distance in order[stripes // 2 - 1 :]]
     early = follow(exchange(early, stripes), *near).reshape(-1, local)
     own, across, second, third = spread_heads(early, far)
     most_shape = (whole, jax.ShapeDtypeStruct(early.shape, jnp.float32))

time: 82.2 us -> 82.4 us (level)
  waiting for transfers between devices: 15.5 us -> 18 us
  starting transfers between devices: 29.1 us -> 27.9 us
  Pallas kernels: 33.4 us -> 32.4 us
    ppermute x16, waiting for transfers between devices: 10.5 us -> 12.2 us  [swap(): lax.ppermute(array, axis_name, [(i, i ^ distance) for i in range(size)])]
    pallas_call x1, Pallas kernels: 21.9 us -> 20.9 us  [project(): pl.pallas_call(functools.partial(project_kernel, halves, levels), grid=(s...]
    all_to_all x2, starting transfers between devices: 12.8 us -> 11.8 us  [exchange(): return lax.all_to_all(array, 'lat', split_axis=0, concat_axis=0, tiled=True)]
    all_to_all x2, waiting for transfers between devices: 4.97 us -> 5.82 us  [exchange(): return lax.all_to_all(array, 'lat', split_axis=0, concat_axis=0, tiled=True)]
  transfers between devices with their start and end apart: 18 -> 18, of which waited for: 8 -> 9; matrix products, arithmetic and copies ran while one was open for 1% -> 1% of each run, Pallas kernels for 35% -> 33%
where the time goes in v1:
time: 82.4 us; the launch traced here: 82 us
  Pallas kernels  32.4 us (39%)
  starting transfers between devices  27.9 us (34%)
  waiting for transfers between devices  18 us (22%)
  local copies, waits for them, and re-layouts  3.68 us (4%)
    pallas_call x1, Pallas kernels, project(): pl.pallas_call(functools.partial(project_kernel, halves, levels), grid=(s...  20.9 us
    ppermute x16, starting transfers between devices, swap(): lax.ppermute(array, axis_name, [(i, i ^ distance) for i in range(size)])  16.1 us
    ppermute x16, waiting for transfers between devices, swap(): lax.ppermute(array, axis_name, [(i, i ^ distance) for i in range(size)])  12.2 us
    all_to_all x2, starting transfers between devices, exchange(): return lax.all_to_all(array, 'lat', split_axis=0, concat_axis=0, tiled=True)  11.8 us
    pallas_call x2, Pallas kernels, attend(): pl.pallas_call(functools.partial(attend_kernel, levels), grid=(steps,), i...  7.63 us
    all_to_all x2, waiting for transfers between devices, exchange(): return lax.all_to_all(array, 'lat', split_axis=0, concat_axis=0, tiled=True)  5.82 us
    pallas_call x2, Pallas kernels, combine(): pl.pallas_call(kernel, in_specs=[pl.BlockSpec(memory_space=pltpu.SMEM)] +...  2.61 us
  transfers between devices with their start and end apart: 18, of which 9 were waited for; matrix products, arithmetic and copies ran while one was open for 1% of the time, Pallas kernels for 33%

profile of v1, /device:TPU:0, one launch (start us, length us, event | category | flops | bytes accessed | tf_op | source)
XLA Modules:
  0.0 82.0 jit_solution(6554091630797785894)
XLA Ops:
  0.0 7.3 %all-to-all-start = ((bf16[8,64,4,256]{3,2,1,0:T(4,128)(2,1)}), bf16[8,64,4,256]{3,2,1,0:T(4,128)(2,1)S(1)}, u32[]{:S(2)}, u32[]{:S(2)}) async-start(bf16[8,64,4,256]{3,2,1,0:T(4,128)(2,1)} %bitcast.11), calls=%async_computation | async-start | bytes 2097152 | tf_op jit(solution)/shard_map/all_to_all | solution.py:320
  7.3 1.1 %constant_dynamic-slice_fusion = (bf16[256,256]{1,0:T(8,128)(2,1)S(1)}, bf16[256,256]{1,0:T(8,128)(2,1)S(1)}, bf16[256,256]{1,0:T(8,128)(2,1)S(1)}, bf16[256,256]{1,0:T(8,128)(2,1)S(1)}) fusion(bf16[256,1024]{1,0:T(8,128)(2,1)} %param.11, s32[]{:T(128)S(6)} %select_n.15, s32[]{:T(128)S(6)} %select_n.13, s32[]{:T(128)S(6)} %select_n.12, s32[]{:T(128)S(6)} %select_n.14), kind=kLoop, calls=%fused_computation | loop fusion | bytes 1048592 | tf_op jit(solution)/shard_map/dynamic_slice | solution.py:328
  8.4 0.7 collective-permute-start.2
  9.1 1.0 %collective-permute-start = (bf16[256,256]{1,0:T(8,128)(2,1)S(1)}, bf16[256,256]{1,0:T(8,128)(2,1)S(1)}, u32[]{:S(2)}, u32[]{:S(2)}) collective-permute-start(bf16[256,256]{1,0:T(8,128)(2,1)S(1)} %get-tuple-element.42), channel_id=1, source_target_pairs={{0,1},{1,0},{2,3},{3,2},{4,5},{5,4},{6,7},{7,6},{8,9},{9,8},{10,11... | collective-permute-start | bytes 393224 | tf_op jit(solution)/shard_map/ppermute | solution.py:306
  10.1 0.5 collective-permute-start.1
  10.6 20.9 %norm_project.1.pair_ref = bf16[8,7,128,512]{3,2,1,0:T(8,128)(2,1)} custom-call(s32[8,64]{1,0:T(8,128)} %bitcast.15, f32[1,1024]{1,0:T(1,128)} %bitcast.16, bf16[1024,256]{1,0:T(8,128)(2,1)} %key_weight_ref.1, bf16[1024,256]{1,0:T(8,128)(2,1)} %value_weight_ref.1, bf16[13,512,1024]{2,1,0:T(8,128)(2,1)} %bitcast.13, bf16[13,512,1024]{2,1,0:T(8,128)(2,1)} %bitcast.14), custom_call_target="tpu_custom_call" | custom-call | flops 20937965568 | bytes 21495808 | tf_op jit(solution)/shard_map/norm_project/pallas_call | solution.py:111
  31.5 1.5 %all-to-all-done = bf16[8,64,4,256]{3,2,1,0:T(4,128)(2,1)S(1)} async-done(((bf16[8,64,4,256]{3,2,1,0:T(4,128)(2,1)}), bf16[8,64,4,256]{3,2,1,0:T(4,128)(2,1)S(1)}, u32[]{:S(2)}, u32[]{:S(2)}) %all-to-all-start) | async-done | bytes 1048608 | tf_op jit(solution)/shard_map/all_to_all | solution.py:320
  33.0 1.1 %reshape.22.query_ref = bf16[8,2,128,256]{3,2,1,0:T(8,128)(2,1)} reshape(bf16[8,64,4,256]{3,2,1,0:T(4,128)(2,1)S(1)} %all-to-all-done) | data formatting | bytes 2097152 | tf_op jit(solution)/shard_map/reshape | solution.py:340
  34.1 3.8 %attend_slots.2.refs_0_ = bf16[1024,256]{1,0:T(8,128)(2,1)} custom-call(bf16[8,2,128,256]{3,2,1,0:T(8,128)(2,1)} %reshape.22.query_ref, bf16[8,7,128,512]{3,2,1,0:T(8,128)(2,1)} %norm_project.1.pair_ref), custom_call_target="tpu_custom_call" | custom-call | flops 3489660928 | bytes 4456448 | tf_op jit(solution)/shard_map/attend_slots/pallas_call | solution.py:195
  38.0 1.5 %collective-permute-start.4 = (bf16[1024,256]{1,0:T(8,128)(2,1)}, bf16[1024,256]{1,0:T(8,128)(2,1)S(1)}, u32[]{:S(2)}, u32[]{:S(2)}) collective-permute-start(bf16[1024,256]{1,0:T(8,128)(2,1)} %attend_slots.2.refs_0_), channel_id=1, source_target_pairs={{0,2},{1,3},{2,0},{3,1},{4,6},{5,7},{6,4},{7,5},{8,10},{9,11},{10,... | collective-permute-start | bytes 1572872 | tf_op jit(solution)/shard_map/ppermute | solution.py:306
  39.5 3.8 %attend_slots.3 = bf16[1024,256]{1,0:T(8,128)(2,1)} custom-call(bf16[8,2,128,256]{3,2,1,0:T(8,128)(2,1)} %reshape.22.query_ref, bf16[8,7,128,512]{3,2,1,0:T(8,128)(2,1)} %norm_project.1.pair_ref, bf16[1024,256]{1,0:T(8,128)(2,1)} %attend_slots.2.refs_0_), custom_call_target="tpu_custom_call" | custom-call | flops 3489660928 | bytes 4456448 | tf_op jit(solution)/shard_map/attend_slots/pallas_call | solution.py:195
  43.3 4.5 %all-to-all-start.1 = ((bf16[8,128,256]{2,1,0:T(8,128)(2,1)}), bf16[8,128,256]{2,1,0:T(8,128)(2,1)S(1)}, u32[]{:S(2)}, u32[]{:S(2)}) async-start(bf16[8,128,256]{2,1,0:T(8,128)(2,1)} %bitcast.12), calls=%async_computation.1 | async-start | bytes 1048576 | tf_op jit(solution)/shard_map/all_to_all | solution.py:320
  47.9 2.5 %collective-permute-done.4.refs_2_ = bf16[1024,256]{1,0:T(8,128)(2,1)S(1)} collective-permute-done((bf16[1024,256]{1,0:T(8,128)(2,1)}, bf16[1024,256]{1,0:T(8,128)(2,1)S(1)}, u32[]{:S(2)}, u32[]{:S(2)}) %collective-permute-start.4) | collective-permute-done | bytes 524320 | tf_op jit(solution)/shard_map/ppermute | solution.py:306
  50.4 1.9 %collective-permute-done.5.refs_3_ = bf16[1024,256]{1,0:T(8,128)(2,1)S(1)} collective-permute-done((bf16[1024,256]{1,0:T(8,128)(2,1)S(1)}, bf16[1024,256]{1,0:T(8,128)(2,1)S(1)}, u32[]{:S(2)}, u32[]{:S(2)}) %collective-permute-start.5) | collective-permute-done | bytes 524320 | tf_op jit(solution)/shard_map/ppermute | solution.py:306
  52.3 1.2 %combine_groups.2 = (bf16[32,4,256]{2,1,0:T(4,128)(2,1)S(1)}, bf16[32,4,256]{2,1,0:T(4,128)(2,1)}, bf16[32,4,256]{2,1,0:T(4,128)(2,1)S(1)}, bf16[32,4,256]{2,1,0...) custom-call(s32[1]{0:T(128)} %bitcast.5.place_ref, ...), custom_call_target="tpu_custom_call" | custom-call | flops 1610612736 | bytes 2621440 | tf_op jit(solution)/shard_map/combine_groups/pallas_call | solution.py:291
  53.5 0.6 copy-done.1
  54.1 2.1 %collective-permute-start.6 = (bf16[32,4,256]{2,1,0:T(4,128)(2,1)}, bf16[32,4,256]{2,1,0:T(4,128)(2,1)S(1)}, u32[]{:S(2)}, u32[]{:S(2)}) collective-permute-start(bf16[32,4,256]{2,1,0:T(4,128)(2,1)} %get-tuple-element.30), channel_id=1, source_target_pairs={{0,4},{4,0},{8,12},{12,8},{16,20},{20,16},{24,28},{28,24},{1,5},{5... | collective-permute-start | bytes 196616 | tf_op jit(solution)/shard_map/ppermute | solution.py:306
  56.2 1.2 %collective-permute-start.7 = (bf16[32,4,256]{2,1,0:T(4,128)(2,1)S(1)}, bf16[32,4,256]{2,1,0:T(4,128)(2,1)S(1)}, u32[]{:S(2)}, u32[]{:S(2)}) collective-permute-start(bf16[32,4,256]{2,1,0:T(4,128)(2,1)S(1)} %get-tuple-element.31), channel_id=1, source_target_pairs={{0,8},{4,12},{8,0},{12,4},{16,24},{20,28},{24,16},{28,20},{1,9},{5... | collective-permute-start | bytes 196616 | tf_op jit(solution)/shard_map/ppermute | solution.py:306
  57.5 0.2 collective-permute-start.8
  57.7 4.3 %all-to-all-done.1 = bf16[8,128,256]{2,1,0:T(8,128)(2,1)S(1)} async-done(((bf16[8,128,256]{2,1,0:T(8,128)(2,1)}), bf16[8,128,256]{2,1,0:T(8,128)(2,1)S(1)}, u32[]{:S(2)}, u32[]{:S(2)}) %all-to-all-start.1) | async-done | bytes 524320 | tf_op jit(solution)/shard_map/all_to_all | solution.py:320
  62.0 0.5 collective-permute-done.7.refs_6_
  62.5 0.9 %collective-permute-done.8.refs_7_ = bf16[32,4,256]{2,1,0:T(4,128)(2,1)S(1)} collective-permute-done((bf16[32,4,256]{2,1,0:T(4,128)(2,1)S(1)}, bf16[32,4,256]{2,1,0:T(4,128)(2,1)S(1)}, u32[]{:S(2)}, u32[]{:S(2)}) %collective-permute-start.8) | collective-permute-done | bytes 65568 | tf_op jit(solution)/shard_map/ppermute | solution.py:306
  63.4 1.1 %collective-permute-start.10 = (bf16[1024,256]{1,0:T(8,128)(2,1)S(1)}, bf16[1024,256]{1,0:T(8,128)(2,1)S(1)}, u32[]{:S(2)}, u32[]{:S(2)}) collective-permute-start(bf16[1024,256]{1,0:T(8,128)(2,1)S(1)} %bitcast.8), channel_id=1, source_target_pairs={{0,2},{1,3},{2,0},{3,1},{4,6},{5,7},{6,4},{7,5},{8,10},{9,11},{10,... | collective-permute-start | bytes 1572872 | tf_op jit(solution)/shard_map/ppermute | solution.py:306
  64.5 2.8 %collective-permute-start.11 = (bf16[32,4,256]{2,1,0:T(4,128)(2,1)S(1)}, bf16[32,4,256]{2,1,0:T(4,128)(2,1)S(1)}, u32[]{:S(2)}, u32[]{:S(2)}) collective-permute-start(bf16[32,4,256]{2,1,0:T(4,128)(2,1)S(1)} %get-tuple-element.34), channel_id=1, source_target_pairs={{0,28},{4,24},{8,20},{12,16},{16,12},{20,8},{24,4},{28,0},{1,29},{... | collective-permute-start | bytes 196616 | tf_op jit(solution)/shard_map/ppermute | solution.py:306
  67.3 2.0 %collective-permute-start.12 = (bf16[32,4,256]{2,1,0:T(4,128)(2,1)S(1)}, bf16[32,4,256]{2,1,0:T(4,128)(2,1)S(1)}, u32[]{:S(2)}, u32[]{:S(2)}) collective-permute-start(bf16[32,4,256]{2,1,0:T(4,128)(2,1)S(1)} %get-tuple-element.35), channel_id=1, source_target_pairs={{0,24},{4,28},{8,16},{12,20},{16,8},{20,12},{24,0},{28,4},{1,25},{... | collective-permute-start | bytes 196616 | tf_op jit(solution)/shard_map/ppermute | solution.py:306
  69.5 2.7 %collective-permute-start.14 = (bf16[32,4,256]{2,1,0:T(4,128)(2,1)S(1)}, bf16[32,4,256]{2,1,0:T(4,128)(2,1)S(1)}, u32[]{:S(2)}, u32[]{:S(2)}) collective-permute-start(bf16[32,4,256]{2,1,0:T(4,128)(2,1)S(1)} %get-tuple-element.37), channel_id=1, source_target_pairs={{0,16},{4,20},{8,24},{12,28},{16,0},{20,4},{24,8},{28,12},{1,17},{... | collective-permute-start | bytes 196616 | tf_op jit(solution)/shard_map/ppermute | solution.py:306
  72.2 1.5 %collective-permute-done.12.refs_10_ = bf16[32,4,256]{2,1,0:T(4,128)(2,1)S(1)} collective-permute-done((bf16[32,4,256]{2,1,0:T(4,128)(2,1)S(1)}, bf16[32,4,256]{2,1,0:T(4,128)(2,1)S(1)}, u32[]{:S(2)}, u32[]{:S(2)}) %collective-permute-start.12) | collective-permute-done | bytes 65568 | tf_op jit(solution)/shard_map/ppermute | solution.py:306
  73.7 4.5 %collective-permute-done.13.refs_9_ = bf16[32,4,256]{2,1,0:T(4,128)(2,1)S(1)} collective-permute-done((bf16[32,4,256]{2,1,0:T(4,128)(2,1)S(1)}, bf16[32,4,256]{2,1,0:T(4,128)(2,1)S(1)}, u32[]{:S(2)}, u32[]{:S(2)}) %collective-permute-start.13) | collective-permute-done | bytes 65568 | tf_op jit(solution)/shard_map/ppermute | solution.py:306
  78.2 0.3 collective-permute-done.14.refs_8_
  78.5 0.8 %copy-done.2 = bf16[32,4,256]{2,1,0:T(4,128)(2,1)S(1)} copy-done((bf16[32,4,256]{2,1,0:T(4,128)(2,1)S(1)}, bf16[32,4,256]{2,1,0:T(4,128)(2,1)}, u32[]{:S(2)}) %copy-start.2) | copy-done | bytes 65560
  79.4 1.4 %combine_groups.3 = (bf16[8,64,4,256]{3,2,1,0:T(4,128)(2,1)}, f32[1024,256]{1,0:T(8,128)S(1)}) custom-call(s32[1]{0:T(128)} %bitcast.5.place_ref, bf16[1024,256]{1,0:T(8,128)(2,1)S(1)} %bitcast.10, bf16[1024,256]{1,0:T(8,128)(2,1)S(1)} %collective-permute-done.10.refs_1_, bf16[256,256]{1,0:T(8,128)(2,1)S(1)} %get-tuple-element.25.refs_4_.refs_2_, ...), custom_call_target="tpu_custom_call" | custom-call | flops 1610612736 | bytes 2621440 | tf_op jit(solution)/shard_map/combine_groups/pallas_call | solution.py:291
  80.8 1.2 %combine_last.1 = bf16[8,64,4,256]{3,2,1,0:T(4,128)(2,1)} custom-call(bf16[1024,256]{1,0:T(8,128)(2,1)S(1)} %collective-permute-done.9.first_ref, bf16[1024,256]{1,0:T(8,128)(2,1)S(1)} %collective-permute-done.15.second_ref, bf16[256,256]{1,0:T(8,128)(2,1)S(1)} %collective-permute-done.refs_5_.first_weight_ref, ...), custom_call_target="tpu_custom_call", output_to_operand_aliasing={{}: (5, {})} | custom-call | flops 805306368 | bytes 2621440 | tf_op jit(solution)/shard_map/combine_last/pallas_call | solution.py:274
  (18 shorter events, 0.3 us)
Async XLA Ops:
  0.0 33.0 %all-to-all-start = ((bf16[8,64,4,256]{3,2,1,0:T(4,128)(2,1)}), bf16[8,64,4,256]{3,2,1,0:T(4,128)(2,1)S(1)}, u32[]{:S(2)}, u32[]{:S(2)}) async-start(bf16[8,64,4,256]{3,2,1,0:T(4,128)(2,1)} %bitcast.11), calls=%async_computation | async-start | bytes 2097152 | tf_op jit(solution)/shard_map/all_to_all | solution.py:320
  8.4 23.1 %collective-permute-start.2 = (bf16[256,256]{1,0:T(8,128)(2,1)S(1)}, bf16[256,256]{1,0:T(8,128)(2,1)S(1)}, u32[]{:S(2)}, u32[]{:S(2)}) collective-permute-start(bf16[256,256]{1,0:T(8,128)(2,1)S(1)} %get-tuple-element.41), channel_id=1, source_target_pairs={{0,3},{1,2},{2,1},{3,0},{4,7},{5,6},{6,5},{7,4},{8,11},{9,10},{10,... | collective-permute-start | bytes 393224 | tf_op jit(solution)/shard_map/ppermute | solution.py:306
  9.1 22.4 %collective-permute-start = (bf16[256,256]{1,0:T(8,128)(2,1)S(1)}, bf16[256,256]{1,0:T(8,128)(2,1)S(1)}, u32[]{:S(2)}, u32[]{:S(2)}) collective-permute-start(bf16[256,256]{1,0:T(8,128)(2,1)S(1)} %get-tuple-element.42), channel_id=1, source_target_pairs={{0,1},{1,0},{2,3},{3,2},{4,5},{5,4},{6,7},{7,6},{8,9},{9,8},{10,11... | collective-permute-start | bytes 393224 | tf_op jit(solution)/shard_map/ppermute | solution.py:306
  10.1 21.4 %collective-permute-start.1 = (bf16[256,256]{1,0:T(8,128)(2,1)S(1)}, bf16[256,256]{1,0:T(8,128)(2,1)S(1)}, u32[]{:S(2)}, u32[]{:S(2)}) collective-permute-start(bf16[256,256]{1,0:T(8,128)(2,1)S(1)} %get-tuple-element.44), channel_id=1, source_target_pairs={{0,2},{1,3},{2,0},{3,1},{4,6},{5,7},{6,4},{7,5},{8,10},{9,11},{10,... | collective-permute-start | bytes 393224 | tf_op jit(solution)/shard_map/ppermute | solution.py:306
  38.0 9.8 %copy-start = (bf16[1024,256]{1,0:T(8,128)(2,1)S(1)}, bf16[1024,256]{1,0:T(8,128)(2,1)}, u32[]{:S(2)}) copy-start(bf16[1024,256]{1,0:T(8,128)(2,1)} %attend_slots.2.refs_0_) | copy-start | bytes 1572868
  38.0 12.4 %collective-permute-start.4 = (bf16[1024,256]{1,0:T(8,128)(2,1)}, bf16[1024,256]{1,0:T(8,128)(2,1)S(1)}, u32[]{:S(2)}, u32[]{:S(2)}) collective-permute-start(bf16[1024,256]{1,0:T(8,128)(2,1)} %attend_slots.2.refs_0_), channel_id=1, source_target_pairs={{0,2},{1,3},{2,0},{3,1},{4,6},{5,7},{6,4},{7,5},{8,10},{9,11},{10,... | collective-permute-start | bytes 1572872 | tf_op jit(solution)/shard_map/ppermute | solution.py:306
  43.3 18.8 %all-to-all-start.1 = ((bf16[8,128,256]{2,1,0:T(8,128)(2,1)}), bf16[8,128,256]{2,1,0:T(8,128)(2,1)S(1)}, u32[]{:S(2)}, u32[]{:S(2)}) async-start(bf16[8,128,256]{2,1,0:T(8,128)(2,1)} %bitcast.12), calls=%async_computation.1 | async-start | bytes 1048576 | tf_op jit(solution)/shard_map/all_to_all | solution.py:320
  47.8 2.6 %collective-permute-start.3 = (bf16[1024,256]{1,0:T(8,128)(2,1)S(1)}, bf16[1024,256]{1,0:T(8,128)(2,1)S(1)}, u32[]{:S(2)}, u32[]{:S(2)}) collective-permute-start(bf16[1024,256]{1,0:T(8,128)(2,1)S(1)} %copy-done), channel_id=1, source_target_pairs={{0,1},{1,0},{2,3},{3,2},{4,5},{5,4},{6,7},{7,6},{8,9},{9,8},{10,11... | collective-permute-start | bytes 1572872 | tf_op jit(solution)/shard_map/ppermute | solution.py:306
  50.4 1.9 %collective-permute-start.5 = (bf16[1024,256]{1,0:T(8,128)(2,1)S(1)}, bf16[1024,256]{1,0:T(8,128)(2,1)S(1)}, u32[]{:S(2)}, u32[]{:S(2)}) collective-permute-start(bf16[1024,256]{1,0:T(8,128)(2,1)S(1)} %collective-permute-done.4.refs_2_), channel_id=1, source_target_pairs={{0,1},{1,0},{2,3},{3,2},{4,5},{5,4},{6,7},{7,6},{8,9},{9,8},{10,11... | collective-permute-start | bytes 1572872 | tf_op jit(solution)/shard_map/ppermute | solution.py:306
  53.5 0.6 copy-start.1
  54.1 7.9 %collective-permute-start.6 = (bf16[32,4,256]{2,1,0:T(4,128)(2,1)}, bf16[32,4,256]{2,1,0:T(4,128)(2,1)S(1)}, u32[]{:S(2)}, u32[]{:S(2)}) collective-permute-start(bf16[32,4,256]{2,1,0:T(4,128)(2,1)} %get-tuple-element.30), channel_id=1, source_target_pairs={{0,4},{4,0},{8,12},{12,8},{16,20},{20,16},{24,28},{28,24},{1,5},{5... | collective-permute-start | bytes 196616 | tf_op jit(solution)/shard_map/ppermute | solution.py:306
  56.2 6.3 %collective-permute-start.7 = (bf16[32,4,256]{2,1,0:T(4,128)(2,1)S(1)}, bf16[32,4,256]{2,1,0:T(4,128)(2,1)S(1)}, u32[]{:S(2)}, u32[]{:S(2)}) collective-permute-start(bf16[32,4,256]{2,1,0:T(4,128)(2,1)S(1)} %get-tuple-element.31), channel_id=1, source_target_pairs={{0,8},{4,12},{8,0},{12,4},{16,24},{20,28},{24,16},{28,20},{1,9},{5... | collective-permute-start | bytes 196616 | tf_op jit(solution)/shard_map/ppermute | solution.py:306
  57.5 5.9 %collective-permute-start.8 = (bf16[32,4,256]{2,1,0:T(4,128)(2,1)S(1)}, bf16[32,4,256]{2,1,0:T(4,128)(2,1)S(1)}, u32[]{:S(2)}, u32[]{:S(2)}) collective-permute-start(bf16[32,4,256]{2,1,0:T(4,128)(2,1)S(1)} %get-tuple-element.32), channel_id=1, source_target_pairs={{0,12},{4,8},{8,4},{12,0},{16,28},{20,24},{24,20},{28,16},{1,13},{... | collective-permute-start | bytes 196616 | tf_op jit(solution)/shard_map/ppermute | solution.py:306
  63.4 15.1 %collective-permute-start.10 = (bf16[1024,256]{1,0:T(8,128)(2,1)S(1)}, bf16[1024,256]{1,0:T(8,128)(2,1)S(1)}, u32[]{:S(2)}, u32[]{:S(2)}) collective-permute-start(bf16[1024,256]{1,0:T(8,128)(2,1)S(1)} %bitcast.8), channel_id=1, source_target_pairs={{0,2},{1,3},{2,0},{3,1},{4,6},{5,7},{6,4},{7,5},{8,10},{9,11},{10,... | collective-permute-start | bytes 1572872 | tf_op jit(solution)/shard_map/ppermute | solution.py:306
  64.5 7.7 %collective-permute-start.11 = (bf16[32,4,256]{2,1,0:T(4,128)(2,1)S(1)}, bf16[32,4,256]{2,1,0:T(4,128)(2,1)S(1)}, u32[]{:S(2)}, u32[]{:S(2)}) collective-permute-start(bf16[32,4,256]{2,1,0:T(4,128)(2,1)S(1)} %get-tuple-element.34), channel_id=1, source_target_pairs={{0,28},{4,24},{8,20},{12,16},{16,12},{20,8},{24,4},{28,0},{1,29},{... | collective-permute-start | bytes 196616 | tf_op jit(solution)/shard_map/ppermute | solution.py:306
  67.3 6.4 %collective-permute-start.12 = (bf16[32,4,256]{2,1,0:T(4,128)(2,1)S(1)}, bf16[32,4,256]{2,1,0:T(4,128)(2,1)S(1)}, u32[]{:S(2)}, u32[]{:S(2)}) collective-permute-start(bf16[32,4,256]{2,1,0:T(4,128)(2,1)S(1)} %get-tuple-element.35), channel_id=1, source_target_pairs={{0,24},{4,28},{8,16},{12,20},{16,8},{20,12},{24,0},{28,4},{1,25},{... | collective-permute-start | bytes 196616 | tf_op jit(solution)/shard_map/ppermute | solution.py:306
  69.2 8.9 %collective-permute-start.13 = (bf16[32,4,256]{2,1,0:T(4,128)(2,1)S(1)}, bf16[32,4,256]{2,1,0:T(4,128)(2,1)S(1)}, u32[]{:S(2)}, u32[]{:S(2)}) collective-permute-start(bf16[32,4,256]{2,1,0:T(4,128)(2,1)S(1)} %get-tuple-element.36), channel_id=1, source_target_pairs={{0,20},{4,16},{8,28},{12,24},{16,4},{20,0},{24,12},{28,8},{1,21},{... | collective-permute-start | bytes 196616 | tf_op jit(solution)/shard_map/ppermute | solution.py:306
  69.5 9.1 %collective-permute-start.14 = (bf16[32,4,256]{2,1,0:T(4,128)(2,1)S(1)}, bf16[32,4,256]{2,1,0:T(4,128)(2,1)S(1)}, u32[]{:S(2)}, u32[]{:S(2)}) collective-permute-start(bf16[32,4,256]{2,1,0:T(4,128)(2,1)S(1)} %get-tuple-element.37), channel_id=1, source_target_pairs={{0,16},{4,20},{8,24},{12,28},{16,0},{20,4},{24,8},{28,12},{1,17},{... | collective-permute-start | bytes 196616 | tf_op jit(solution)/shard_map/ppermute | solution.py:306
  72.2 8.6 %collective-permute-start.9 = (bf16[1024,256]{1,0:T(8,128)(2,1)S(1)}, bf16[1024,256]{1,0:T(8,128)(2,1)S(1)}, u32[]{:S(2)}, u32[]{:S(2)}) collective-permute-start(bf16[1024,256]{1,0:T(8,128)(2,1)S(1)} %bitcast.9), channel_id=1, source_target_pairs={{0,1},{1,0},{2,3},{3,2},{4,5},{5,4},{6,7},{7,6},{8,9},{9,8},{10,11... | collective-permute-start | bytes 1572872 | tf_op jit(solution)/shard_map/ppermute | solution.py:306
  78.5 2.3 %collective-permute-start.15 = (bf16[1024,256]{1,0:T(8,128)(2,1)S(1)}, bf16[1024,256]{1,0:T(8,128)(2,1)S(1)}, u32[]{:S(2)}, u32[]{:S(2)}) collective-permute-start(bf16[1024,256]{1,0:T(8,128)(2,1)S(1)} %collective-permute-done.10.refs_1_), channel_id=1, source_target_pairs={{0,1},{1,0},{2,3},{3,2},{4,5},{5,4},{6,7},{7,6},{8,9},{9,8},{10,11... | collective-permute-start | bytes 1572872 | tf_op jit(solution)/shard_map/ppermute | solution.py:306
  78.5 0.8 %copy-start.2 = (bf16[32,4,256]{2,1,0:T(4,128)(2,1)S(1)}, bf16[32,4,256]{2,1,0:T(4,128)(2,1)}, u32[]{:S(2)}) copy-start(bf16[32,4,256]{2,1,0:T(4,128)(2,1)} %copy-done.1) | copy-start | bytes 196612
